TPU v7x, 32 devices: a whole 2x2x4 slice. The times are simulated.
32 devices in a mesh: parts: 2 (over y), own: 4 (over z), dp: 2 (over x), sub: 2 (over core).
Axes of the slice: x: 2, y: 2, z: 4, core: 2. Of those that a mesh axis runs over, the one named last changes fastest.
Arguments:
- grad_partials: bfloat16 [4, 2, 4, 2, 4, 64, 512], P(('parts', 'dp'), None, None, 'sub', 'own'), parts along dimension 0
- owner_table: int32 [4, 4, 1], P('parts'), parts along dimension 0, may hold values from 0 to 3; in each aligned block of 4 rows (0 to 3, 4 to 7, ..., all dimensions but the last counted through in order) at most 2 rows name the same one
- left_factor: float32 [4, 4, 2, 512, 512], P(('parts', 'dp'), 'own', None, 'sub'), parts along dimension 0, as said below
- right_factor: float32 [4, 4, 2, 512, 512], P(('parts', 'dp'), 'own', None, 'sub'), parts along dimension 0, as said below
- left_root: float32 [4, 4, 2, 512, 512], P(('parts', 'dp'), 'own', None, 'sub'), parts along dimension 0, as said below
- right_root: float32 [4, 4, 2, 512, 512], P(('parts', 'dp'), 'own', None, 'sub'), parts along dimension 0, as said below
Outputs:
- update: bfloat16 [4, 4, 2, 4, 64, 512], P(('parts', 'dp'), None, 'sub', 'own'), parts along dimension 0
- new_left: float32 [4, 4, 2, 512, 512], P(('parts', 'dp'), 'own', None, 'sub'), parts along dimension 0
- new_right: float32 [4, 4, 2, 512, 512], P(('parts', 'dp'), 'own', None, 'sub'), parts along dimension 0
There are 2 independent parts, one for each index of `parts`. A program takes and returns all parts, laid end to end along the dimension named above; each array names one. Nothing has to cross between parts.
Inputs may be any that keep to these rules, and one draw needn't show every extreme that they name: owner_table[d, j, 0] owns block j of column d; no owner gets more than 2 blocks of one column, and in some column one owner gets exactly 2. `left_factor`: every 512 x 512 block is symmetric. `right_factor`: every 512 x 512 block is symmetric. `left_root`: every 512 x 512 block is symmetric. `right_root`: every 512 x 512 block is symmetric.
All inputs are finite; a program needn't handle non-finite values.
Results may differ from a plain program's by a relative error of at most 0.0053.
Values may be sent and summed in bfloat16 or wider, within the bound.
A program may use at most 64 MiB of HBM per device.

v0:
```python
import jax
import jax.numpy as jnp
from jax import lax
from jax.sharding import PartitionSpec as P

BETA = 0.9
EPS = 1e-06


def ranking(owners):
    count = owners.shape[0]
    later = lax.broadcasted_iota(jnp.int32, (count, count), 0)
    sooner = lax.broadcasted_iota(jnp.int32, (count, count), 1)
    same = (owners[:, None] == owners[None, :]) & (sooner < later)
    return jnp.sum(same.astype(jnp.int32), axis=1)


def on_device(grad_partials, owner_table, left_factor, right_factor, left_root, right_root):
    column_id = lax.axis_index("dp")
    owner_id = lax.axis_index("own")
    half_id = lax.axis_index("sub")
    peers = lax.axis_size("own")
    summed = lax.psum_scatter(
        grad_partials.astype(jnp.float32).astype(jnp.bfloat16),
        "dp",
        scatter_dimension=1,
        tiled=True,
    ).astype(jnp.float32)
    count = summed.shape[2]
    piece_rows = summed.shape[5]
    order = summed.shape[6]
    mine = summed.reshape(count, piece_rows, order).astype(jnp.bfloat16)
    owners = lax.dynamic_index_in_dim(owner_table, column_id, 0, keepdims=False)[:, 0]
    ranks = ranking(owners)
    slots = left_factor.shape[2]
    owner_grid = lax.broadcasted_iota(jnp.int32, (peers, slots, count), 0)
    slot_grid = lax.broadcasted_iota(jnp.int32, (peers, slots, count), 1)
    select = ((owners[None, None, :] == owner_grid) & (ranks[None, None, :] == slot_grid)).astype(
        jnp.bfloat16
    )
    picks = lax.dynamic_index_in_dim(select, owner_id, 0, keepdims=False)
    taken = jnp.einsum(
        "mj,jnrc->mnrc",
        picks,
        lax.all_gather(mine[:, None], "own", axis=1, tiled=True),
        preferred_element_type=jnp.float32,
    ).astype(jnp.bfloat16)
    rows = peers * piece_rows
    assigned = taken.reshape(slots, rows, order)
    whole = lax.all_gather(assigned, "sub", axis=1, tiled=True)
    wide = whole.astype(jnp.float32)
    left_new = BETA * left_factor[0, 0] + (1.0 - BETA) / order * jnp.einsum(
        "srk,sck->src", assigned, whole, preferred_element_type=jnp.float32
    )
    side = lax.dynamic_slice_in_dim(whole, half_id * rows, rows, 2)
    right_new = BETA * right_factor[0, 0] + (1.0 - BETA) / order * jnp.einsum(
        "sic,sik->sck", side, whole, preferred_element_type=jnp.float32
    )
    image_part = jnp.einsum("sik,sck->sic", wide, right_root[0, 0], precision=lax.Precision.HIGHEST)
    image = lax.all_gather(image_part, "sub", axis=2, tiled=True)
    precond = jnp.einsum("srk,skc->src", left_root[0, 0], image, precision=lax.Precision.HIGHEST)
    total = order * order
    grad_sq = jnp.sum(wide * wide, axis=(1, 2))
    pre_sq = lax.psum(jnp.sum(precond * precond, axis=(1, 2)), "sub")
    graft = jnp.sqrt(grad_sq / total) / jnp.sqrt(pre_sq / total + EPS)
    scaled = (precond * graft[:, None, None]).astype(jnp.bfloat16)
    returned = lax.all_to_all(
        scaled.reshape(slots, peers, piece_rows, order),
        "own",
        split_axis=1,
        concat_axis=1,
        tiled=True,
    )
    update = jnp.einsum(
        "wmj,mwrc->jrc", select, returned, preferred_element_type=jnp.float32
    ).astype(jnp.bfloat16)
    return (
        update.reshape(1, count, 1, 1, piece_rows, order),
        left_new.reshape(1, 1, slots, rows, order),
        right_new.reshape(1, 1, slots, rows, order),
    )


def solution(mesh):
    return jax.shard_map(
        on_device,
        mesh=mesh,
        in_specs=(
            P(("parts", "dp"), None, None, "sub", "own", None, None),
            P("parts", None, None),
            P(("parts", "dp"), "own", None, "sub", None),
            P(("parts", "dp"), "own", None, "sub", None),
            P(("parts", "dp"), "own", None, "sub", None),
            P(("parts", "dp"), "own", None, "sub", None),
        ),
        out_specs=(
            P(("parts", "dp"), None, "sub", "own", None, None),
            P(("parts", "dp"), "own", None, "sub", None),
            P(("parts", "dp"), "own", None, "sub", None),
        ),
        check_vma=False,
    )
```

profile of v0, /device:TPU:1, one launch (start us, length us, event | category | flops | bytes accessed | tf_op | source)
XLA Modules:
  0.0 119.5 jit_solution(4891162897961052839)
XLA Ops:
  7.2 0.7 reduce-scatter.2.cloned.1.call-update
  8.0 19.0 %reduce-scatter.2.cloned.1.call-done = bf16[1,1,4,1,1,64,512]{6,5,4,3,2,0,1:T(8,128)(2,1)} async-done(((bf16[1,2,4,1,1,64,512]{6,5,4,3,2,0,1:T(8,128)(2,1)}), bf16[1,1,4,1,1,64,512]{6,5,4,3,2,0,1:T(8,128)(2,1)}) %reduce-scatter.2.cloned.1.call-update) | async-done | bytes 262160 | tf_op jit(solution)/shard_map/reduce_scatter | solution.py:23
  27.0 0.0 all-gather.5.cloned.1.call-start
  27.0 0.7 fusion.19
  27.7 0.2 convert_reduce_fusion
  27.9 28.5 %all-gather.9.cloned.1.call-done = bf16[1,1,4,4,1,64,512]{6,5,4,2,1,0,3:T(8,128)(2,1)} async-done(((bf16[1,1,4,1,1,64,512]{6,5,4,2,1,0,3:T(8,128)(2,1)}), bf16[1,1,4,4,1,64,512]{6,5,4,2,1,0,3:T(8,128)(2,1)}) %all-gather.9.cloned.1.call-update) | async-done | bytes 1048592 | tf_op jit(solution)/shard_map/all_gather | solution.py:45
  56.4 2.1 %convolution_convert_fusion = bf16[2,4,64,512]{3,0,2,1:T(2,128)(2,1)S(1)} fusion(bf16[1,1,4,4,1,64,512]{6,5,4,2,1,0,3:T(8,128)(2,1)} %all-gather.9.cloned.1.call-done, pred[4,2,4]{2,1,0:T(4,128)(4,1)S(1)} %compare_and_fusion, s32[]{:T(128)S(6)} %select_n.12), kind=kOutput, calls=%fused_computation.7 | convolution fusion | flops 2359296 | bytes 1573380 | tf_op jit(solution)/shard_map/mj,jnrc->mnrc/dot_general | solution.py:42
  58.5 0.8 copy-done.2
  59.3 0.8 copy.29
  60.2 0.0 all-gather.7.cloned.1.call-start
  60.2 9.1 %all-gather.5.cloned.1.call-done = bf16[2,512,512]{2,1,0:T(8,128)(2,1)} async-done(((bf16[2,256,512]{2,1,0:T(8,128)(2,1)}), bf16[2,512,512]{2,1,0:T(8,128)(2,1)}) %all-gather.5.cloned.1.call-update) | async-done | bytes 1048592 | tf_op jit(solution)/shard_map/all_gather | solution.py:50
  69.4 3.3 %fusion.8 = f32[2,512,256]{2,1,0:T(8,128)} fusion(bf16[2,512,512]{2,1,0:T(8,128)(2,1)} %all-gather.5.cloned.1.call-done, f32[1,1,2,256,512]{4,3,2,1,0:T(8,128)S(1)} %copy-done.4), kind=kOutput, calls=%fused_computation.13 | convolution fusion | flops 1610612736 | bytes 3145728 | tf_op jit(solution)/shard_map/sik,sck->sic/dot_general | solution.py:59
  72.8 0.4 multiply_reduce_fusion
  73.2 11.5 %all-gather.7.cloned.1.call-done = f32[2,512,512]{2,1,0:T(8,128)} async-done(((f32[2,512,256]{2,1,0:T(8,128)}), f32[2,512,512]{2,1,0:T(8,128)}) %all-gather.7.cloned.1.call-update) | async-done | bytes 2097168 | tf_op jit(solution)/shard_map/all_gather | solution.py:60
  84.7 3.8 %multiply_reduce_fusion.1 = (f32[2]{0:T(128)S(1)}, f32[2,512,256]{1,2,0:T(8,128)S(1)}) fusion(f32[2,512,512]{2,1,0:T(8,128)} %all-gather.7.cloned.1.call-done, f32[1,1,2,256,512]{4,3,2,1,0:T(8,128)S(1)} %copy-done), kind=kOutput, calls=%fused_computation.18 | convolution fusion | flops 1611137024 | bytes 4194312 | tf_op jit(solution)/shard_map/srk,skc->src/dot_general | solution.py:61
  88.5 2.5 %psum.7 = f32[2]{0:T(128)S(1)} all-reduce(f32[2]{0:T(128)S(1)} %get-tuple-element.12), channel_id=1, replica_groups=mesh['parts'=2,'own'=4,'dp'=2,'sub'=2] {'sub'}, use_global_device_ids=true, to_apply=%region_4.5 | all-reduce | flops 2 | bytes 16 | tf_op jit(solution)/shard_map/psum | solution.py:64
  90.9 0.2 multiply_convert_fusion
  91.1 1.3 %copy.30 = bf16[2,4,64,512]{3,0,2,1:T(2,128)(2,1)} copy(bf16[2,4,64,512]{3,2,1,0:T(8,128)(2,1)S(1)} %bitcast.57) | data formatting | bytes 1048576 | tf_op jit(solution)/shard_map/reshape | solution.py:68
  92.4 4.8 %all-to-all-start = ((bf16[2,4,64,512]{3,0,2,1:T(2,128)(2,1)}), bf16[2,4,64,512]{3,0,2,1:T(2,128)(2,1)S(1)}, u32[]{:S(2)}, u32[]{:S(2)}) async-start(bf16[2,4,64,512]{3,0,2,1:T(2,128)(2,1)} %copy.30), calls=%async_computation.1 | async-start | bytes 1048576 | tf_op jit(solution)/shard_map/all_to_all | solution.py:67
  97.2 2.8 %fusion.1 = f32[1,1,2,256,512]{4,3,2,1,0:T(8,128)} fusion(bf16[2,512,512]{2,1,0:T(8,128)(2,1)S(1)} %copy-done.1, f32[1,1,2,256,512]{4,3,2,1,0:T(8,128)} %param.9, s32[]{:T(128)S(6)} %select_n.13), kind=kOutput, calls=%fused_computation.3 | convolution fusion | flops 269221888 | bytes 3670020 | tf_op jit(solution)/shard_map/sic,sik->sck/dot_general | solution.py:56
  100.0 1.5 %fusion.3 = f32[1,1,2,256,512]{4,3,2,1,0:T(8,128)} fusion(bf16[2,512,512]{2,1,0:T(8,128)(2,1)S(1)} %copy-done.1, f32[1,1,2,256,512]{4,3,2,1,0:T(8,128)S(1)} %copy-done.5, bf16[2,256,512]{2,0,1:T(2,128)(2,1)S(1)} %bitcast.56), kind=kOutput, calls=%fused_computation.6 | convolution fusion | flops 269221888 | bytes 3670016 | tf_op jit(solution)/shard_map/srk,sck->src/dot_general | solution.py:52
  101.5 9.9 %all-to-all-done = bf16[2,4,64,512]{3,0,2,1:T(2,128)(2,1)S(1)} async-done(((bf16[2,4,64,512]{3,0,2,1:T(2,128)(2,1)}), bf16[2,4,64,512]{3,0,2,1:T(2,128)(2,1)S(1)}, u32[]{:S(2)}, u32[]{:S(2)}) %all-to-all-start) | async-done | bytes 524320 | tf_op jit(solution)/shard_map/all_to_all | solution.py:67
  111.4 0.9 fusion.5
  112.2 0.8 copy.34
  (18 shorter events, 0.2 us)
Async XLA Ops:
  7.2 77.5 %copy-start = (f32[1,1,2,256,512]{4,3,2,1,0:T(8,128)S(1)}, f32[1,1,2,256,512]{4,3,2,1,0:T(8,128)}, u32[]{:S(2)}) copy-start(f32[1,1,2,256,512]{4,3,2,1,0:T(8,128)} %param.10) | copy-start | bytes 3145732
  7.2 19.7 %reduce-scatter.2.cloned.1.call-start = ((), (), s32[]{:S(2)}) async-start(), calls=%async_computation.2 | async-start | bytes 786432 | tf_op jit(solution)/shard_map/reduce_scatter | solution.py:23
  7.9 48.5 %all-gather.9.cloned.1.call-start = ((), (), s32[]{:S(2)}) async-start(), calls=%async_computation.5 | async-start | bytes 1310720 | tf_op jit(solution)/shard_map/all_gather | solution.py:45
  26.9 42.4 %copy-start.4 = (f32[1,1,2,256,512]{4,3,2,1,0:T(8,128)S(1)}, f32[1,1,2,256,512]{4,3,2,1,0:T(8,128)}, u32[]{:S(2)}) copy-start(f32[1,1,2,256,512]{4,3,2,1,0:T(8,128)} %param.11) | copy-start | bytes 3145732
  27.0 42.4 %all-gather.5.cloned.1.call-start = ((), (), s32[]{:S(2)}) async-start(), calls=%async_computation.3 | async-start | bytes 1572864 | tf_op jit(solution)/shard_map/all_gather | solution.py:50
  58.5 0.8 copy-start.2
  60.2 24.5 %all-gather.7.cloned.1.call-start = ((), (), s32[]{:S(2)}) async-start(), calls=%async_computation.4 | async-start | bytes 3145728 | tf_op jit(solution)/shard_map/all_gather | solution.py:60
  69.4 3.4 %copy-start.1 = (bf16[2,512,512]{2,1,0:T(8,128)(2,1)S(1)}, bf16[2,512,512]{2,1,0:T(8,128)(2,1)}, u32[]{:S(2)}) copy-start(bf16[2,512,512]{2,1,0:T(8,128)(2,1)} %all-gather.5.cloned.1.call-done) | copy-start | bytes 3145732
  92.4 7.6 %copy-start.3 = (bf16[2,4,64,512]{3,0,2,1:T(2,128)(2,1)S(1)}, bf16[2,4,64,512]{3,0,2,1:T(2,128)(2,1)}, u32[]{:S(2)}) copy-start(bf16[2,4,64,512]{3,0,2,1:T(2,128)(2,1)} %copy-done.2) | copy-start | bytes 1572868
  92.4 18.9 %all-to-all-start = ((bf16[2,4,64,512]{3,0,2,1:T(2,128)(2,1)}), bf16[2,4,64,512]{3,0,2,1:T(2,128)(2,1)S(1)}, u32[]{:S(2)}, u32[]{:S(2)}) async-start(bf16[2,4,64,512]{3,0,2,1:T(2,128)(2,1)} %copy.30), calls=%async_computation.1 | async-start | bytes 1048576 | tf_op jit(solution)/shard_map/all_to_all | solution.py:67
  97.2 2.8 %copy-start.5 = (f32[1,1,2,256,512]{4,3,2,1,0:T(8,128)S(1)}, f32[1,1,2,256,512]{4,3,2,1,0:T(8,128)}, u32[]{:S(2)}) copy-start(f32[1,1,2,256,512]{4,3,2,1,0:T(8,128)} %param.8) | copy-start | bytes 3145732
Sparse Core Ops, SparseCore 0:
  10.3 16.6 reduce-scatter.1
  28.6 27.7 all-gather.8
  60.3 9.0 all-gather.4
  72.9 11.7 all-gather.6
where the time goes:
time: 121 us; the launch traced here: 120 us
  waiting for transfers between devices  78.7 us (65%)
  matrix products  14.4 us (12%)
  between operations  13.8 us (11%)
  starting transfers between devices  4.95 us (4%)
  local copies, waits for them, and re-layouts  4.48 us (4%)
  blocking collectives  2.46 us (2%)
    all_gather x1, waiting for transfers between devices, on_device(): lax.all_gather(mine[:, None], 'own', axis=1, tiled=True)  28.5 us
    reduce_scatter x1, waiting for transfers between devices, on_device(): lax.psum_scatter(grad_partials.astype(jnp.float32).astype(jnp.bfloat16),...  19 us
    all_gather x1, waiting for transfers between devices, on_device(): image = lax.all_gather(image_part, 'sub', axis=2, tiled=True)  11.5 us
    all_to_all x1, waiting for transfers between devices, on_device(): lax.all_to_all(scaled.reshape(slots, peers, piece_rows, order), 'own', sp...  9.87 us
    all_gather x1, waiting for transfers between devices, on_device(): whole = lax.all_gather(assigned, 'sub', axis=1, tiled=True)  9.14 us
    all_to_all x1, starting transfers between devices, on_device(): lax.all_to_all(scaled.reshape(slots, peers, piece_rows, order), 'own', sp...  4.8 us
    dot_general x1, matrix products, on_device(): jnp.einsum('srk,skc->src', left_root[0, 0], image, precision=lax.Precisio...  3.8 us
    dot_general x1, matrix products, on_device(): jnp.einsum('sik,sck->sic', wide, right_root[0, 0], precision=lax.Precisio...  3.34 us
  transfers between devices with their start and end apart: 5, of which 5 were waited for; matrix products, arithmetic and copies ran while one was open for 5% of the time, Pallas kernels for 0%

commit v1 on v0

v1 whole, which is shorter than its diff:
```python
import functools

import jax
import jax.numpy as jnp
from jax import lax
from jax.experimental import pallas as pl
from jax.experimental.pallas import tpu as pltpu
from jax.sharding import PartitionSpec as P

BETA = 0.9
EPS = 1e-06
F32 = jnp.float32
BF16 = jnp.bfloat16
NT = (((1,), (1,)), ((), ()))
TN = (((0,), (0,)), ((), ()))
MESH = pl.DeviceIdType.MESH


def kernel(
    own, dp, sub, count, piece, order, slots, chunk,
    g_hbm, table, lf_hbm, rf_hbm, lr_hbm, rr_hbm,
    up_ref, nl_hbm, nr_hbm,
    g_mine, g_peer, outbox, whole, left, right, left_hi, left_lo, right_hi, right_lo,
    image_hi, image_lo, precond, lf, rf, back, inbox, sq_out, sq_in,
    load_sem, store_sem, dp_send, dp_recv, own_send, own_recv, sub_send, sub_recv,
    root_send, root_recv, back_send, back_recv, sq_send, sq_recv,
):
    me_own, me_dp, me_sub = lax.axis_index("own"), lax.axis_index("dp"), lax.axis_index("sub")
    half = order // sub
    chunks = piece // chunk

    def row0(h, p):
        return pl.multiple_of((h * own + p) * piece, piece)

    loads = []

    def load(src, dst):
        copy = pltpu.make_async_copy(src, dst, load_sem.at[len(loads)])
        copy.start()
        loads.append(copy)
        return copy

    mine = load(g_hbm.at[me_dp], g_mine)

    barrier = pltpu.get_barrier_semaphore()
    greeted = 0
    for k in range(1, dp):
        pl.semaphore_signal(barrier, inc=1, device_id={"dp": lax.rem(me_dp + k, dp)}, device_id_type=MESH)
        greeted += 1
    pairs = [(ko, ks) for ko in range(own) for ks in range(sub) if ko or ks]
    for ko, ks in pairs:
        pl.semaphore_signal(
            barrier, inc=1,
            device_id={"own": lax.rem(me_own + ko, own), "sub": lax.rem(me_sub + ks, sub)},
            device_id_type=MESH,
        )
        greeted += 1

    right_load = load(rr_hbm, right)
    my_half = pl.ds(pl.multiple_of(me_sub * half, half), half)
    left_load = load(lr_hbm, left.at[:, my_half, :])
    lf_load = load(lf_hbm, lf)
    rf_load = load(rf_hbm, rf)

    owner = [table[me_dp, j] for j in range(count)]
    rank = []
    for j in range(count):
        r = jnp.int32(0)
        for j2 in range(j):
            r = r + jnp.where(owner[j2] == owner[j], 1, 0).astype(jnp.int32)
        rank.append(r)

    pl.semaphore_wait(barrier, greeted)

    sends = []

    def remote(src, dst, send, recv, to):
        copy = pltpu.make_async_remote_copy(
            src_ref=src, dst_ref=dst, send_sem=send, recv_sem=recv, device_id=to, device_id_type=MESH
        )
        copy.start()
        sends.append(copy)
        return copy

    dp_copies = {}
    for c in range(chunks):
        for k in range(1, dp):
            to = lax.rem(me_dp + k, dp)
            dp_copies[c, k] = remote(
                g_hbm.at[to, :, pl.ds(c * chunk, chunk), :],
                g_peer.at[k - 1, :, pl.ds(c * chunk, chunk), :],
                dp_send.at[c, k - 1], dp_recv.at[c, k - 1], {"dp": to},
            )
    root_copies = [
        remote(
            lr_hbm, left.at[:, my_half, :], root_send.at[k - 1], root_recv.at[k - 1],
            {"sub": lax.rem(me_sub + k, sub)},
        )
        for k in range(1, sub)
    ]

    far_first = sorted(range(1, own), key=lambda k: -min(k, own - k))
    own_copies, sub_copies = {}, {}

    def forward(m, p, c, k):
        rows = pl.ds(pl.multiple_of(row0(me_sub, p) + c * chunk, chunk), chunk)
        for ks in range(1, sub):
            sub_copies[m, c, k, ks] = remote(
                whole.at[m, rows, :], whole.at[m, rows, :],
                sub_send.at[m, c, k, ks - 1], sub_recv.at[m, c, k, ks - 1],
                {"sub": lax.rem(me_sub + ks, sub)},
            )

    def dispatch(m, c):
        for k in far_first:
            to = lax.rem(me_own + k, own)
            rows = pl.ds(pl.multiple_of(row0(me_sub, me_own) + c * chunk, chunk), chunk)
            own_copies[m, c, k] = remote(
                outbox.at[m, k - 1, pl.ds(c * chunk, chunk), :], whole.at[m, rows, :],
                own_send.at[m, c, k - 1], own_recv.at[m, c, k - 1], {"own": to},
            )
        forward(m, me_own, c, 0)

    mine.wait()
    for c in range(chunks):
        rows = pl.ds(c * chunk, chunk)
        for k in range(1, dp):
            dp_copies[c, k].wait_recv()
        blocks = []
        for j in range(count):
            total = g_mine[j, rows, :].astype(F32)
            for k in range(1, dp):
                total = total + g_peer[k - 1, j, rows, :].astype(F32)
            blocks.append(total.astype(BF16))
        for m in range(slots):
            for k in range(own):
                w = lax.rem(me_own + k, own)
                value = jnp.zeros((chunk, order), BF16)
                for j in range(count):
                    value = jnp.where((owner[j] == w) & (rank[j] == m), blocks[j], value)
                if k:
                    outbox[m, k - 1, rows, :] = value
                else:
                    at = pl.ds(pl.multiple_of(row0(me_sub, me_own) + c * chunk, chunk), chunk)
                    whole[m, at, :] = value
            if m == 0:
                dispatch(0, c)
    for m in range(1, slots):
        for c in range(chunks):
            dispatch(m, c)

    right_load.wait()
    for m in range(slots):
        value = right[m]
        hi = value.astype(BF16)
        right_hi[m] = hi
        right_lo[m] = (value - hi.astype(F32)).astype(BF16)
    left_load.wait()
    for copy in root_copies:
        copy.wait_recv()
    for m in range(slots):
        value = left[m]
        hi = value.astype(BF16)
        left_hi[m] = hi
        left_lo[m] = (value - hi.astype(F32)).astype(BF16)

    entries = order * order
    stores, back_copies = [], {}
    near_first = sorted(range(1, own), key=lambda k: min(k, own - k))
    for m in range(slots):
        for c in range(chunks):
            for k in near_first:
                own_copies[m, c, k].wait_recv()
                forward(m, lax.rem(me_own - k + own, own), c, k)
        for c in range(chunks):
            for k in [0] + near_first:
                for ks in range(1, sub):
                    sub_copies[m, c, k, ks].wait_recv()
        block = whole[m]
        image = lax.dot_general(block, right_hi[m], NT, preferred_element_type=F32)
        image = image + lax.dot_general(block, right_lo[m], NT, preferred_element_type=F32)
        hi = image.astype(BF16)
        image_hi[...] = hi
        image_lo[...] = (image - hi.astype(F32)).astype(BF16)
        pre = jnp.dot(left_hi[m], image_hi[...], preferred_element_type=F32)
        pre = pre + jnp.dot(left_hi[m], image_lo[...], preferred_element_type=F32)
        pre = pre + jnp.dot(left_lo[m], image_hi[...], preferred_element_type=F32)
        precond[...] = pre
        pre_sq = jnp.sum(jnp.sum(pre * pre, axis=0, keepdims=True), axis=1, keepdims=True)
        sq_out[m] = jnp.broadcast_to(pre_sq, (8, 128))
        sq_copies = [
            remote(
                sq_out.at[m], sq_in.at[m, k - 1], sq_send.at[m, k - 1], sq_recv.at[m, k - 1],
                {"sub": lax.rem(me_sub + k, sub)},
            )
            for k in range(1, sub)
        ]
        wide = whole[m].astype(F32)
        grad_sq = jnp.sum(jnp.sum(wide * wide, axis=0, keepdims=True), axis=1, keepdims=True)
        for k in range(1, sub):
            sq_copies[k - 1].wait_recv()
            pre_sq = pre_sq + sq_in[m, k - 1, 0:1, 0:1]
        graft = jnp.sqrt(grad_sq / entries) / jnp.sqrt(pre_sq / entries + EPS)
        back[m] = (precond[...] * graft).astype(BF16)
        for ko in far_first + [0]:
            for ks in range(sub):
                if not (ko or ks):
                    continue
                p, h = lax.rem(me_own + ko, own), lax.rem(me_sub + ks, sub)
                back_copies[m, ko, ks] = remote(
                    back.at[m, pl.ds(row0(h, p), piece), :], inbox.at[me_own, m, me_sub],
                    back_send.at[m, ko, ks], back_recv.at[m, ko, ks], {"own": p, "sub": h},
                )
        inbox[me_own, m, me_sub] = back[m, pl.ds(row0(me_sub, me_own), piece), :]

        if m == 0:
            lf_load.wait()
            rf_load.wait()
        block = whole[m]
        lf[m] = BETA * lf[m] + (1.0 - BETA) / order * lax.dot_general(
            whole[m, my_half, :], block, NT, preferred_element_type=F32
        )
        rf[m] = BETA * rf[m] + (1.0 - BETA) / order * lax.dot_general(
            whole[m, :, my_half], block, TN, preferred_element_type=F32
        )
        for i, (src, dst) in enumerate(((lf, nl_hbm), (rf, nr_hbm))):
            copy = pltpu.make_async_copy(src.at[m], dst.at[m], store_sem.at[m, i])
            copy.start()
            stores.append(copy)

    for copy in back_copies.values():
        copy.wait_recv()
    for j in range(count):
        for c in range(sub):
            up_ref[j, :, c * half:(c + 1) * half] = inbox[owner[j], jnp.minimum(rank[j], slots - 1), c]
    for copy in sends:
        copy.wait_send()
    for copy in stores:
        copy.wait()


def on_device(grad_partials, owner_table, left_factor, right_factor, left_root, right_root):
    own, dp, sub = lax.axis_size("own"), lax.axis_size("dp"), lax.axis_size("sub")
    count, piece, order = grad_partials.shape[2], grad_partials.shape[5], grad_partials.shape[6]
    slots = left_factor.shape[2]
    half = order // sub
    chunk = 16 if piece % 16 == 0 else piece
    chunks = piece // chunk
    factor = (slots, half, order)
    dma = pltpu.SemaphoreType.DMA
    hbm, vmem = pl.BlockSpec(memory_space=pl.ANY), pl.BlockSpec(memory_space=pltpu.VMEM)
    peers = max(own - 1, 1)
    twins = max(sub - 1, 1)
    update, new_left, new_right = pl.pallas_call(
        functools.partial(kernel, own, dp, sub, count, piece, order, slots, chunk),
        out_shape=(
            jax.ShapeDtypeStruct((count, piece, order), BF16),
            jax.ShapeDtypeStruct(factor, F32),
            jax.ShapeDtypeStruct(factor, F32),
        ),
        in_specs=[hbm, pl.BlockSpec(memory_space=pltpu.SMEM), hbm, hbm, hbm, hbm],
        out_specs=(vmem, hbm, hbm),
        scratch_shapes=[
            pltpu.VMEM((count, piece, order), BF16),
            pltpu.VMEM((max(dp - 1, 1), count, piece, order), BF16),
            pltpu.VMEM((slots, peers, piece, order), BF16),
            pltpu.VMEM((slots, order, order), BF16),
            pltpu.VMEM((slots, order, order), F32),
            pltpu.VMEM(factor, F32),
            pltpu.VMEM((slots, order, order), BF16),
            pltpu.VMEM((slots, order, order), BF16),
            pltpu.VMEM(factor, BF16),
            pltpu.VMEM(factor, BF16),
            pltpu.VMEM((order, half), BF16),
            pltpu.VMEM((order, half), BF16),
            pltpu.VMEM((order, half), F32),
            pltpu.VMEM(factor, F32),
            pltpu.VMEM(factor, F32),
            pltpu.VMEM((slots, order, half), BF16),
            pltpu.VMEM((own, slots, sub, piece, half), BF16),
            pltpu.VMEM((slots, 8, 128), F32),
            pltpu.VMEM((slots, twins, 8, 128), F32),
            dma((5,)),
            dma((slots, 2)),
            dma((chunks, max(dp - 1, 1))),
            dma((chunks, max(dp - 1, 1))),
            dma((slots, chunks, peers)),
            dma((slots, chunks, peers)),
            dma((slots, chunks, own, twins)),
            dma((slots, chunks, own, twins)),
            dma((twins,)),
            dma((twins,)),
            dma((slots, own, sub)),
            dma((slots, own, sub)),
            dma((slots, twins)),
            dma((slots, twins)),
        ],
        compiler_params=pltpu.CompilerParams(
            collective_id=0, has_side_effects=True, vmem_limit_bytes=48 * 1024 * 1024
        ),
    )(
        grad_partials.reshape(dp, count, piece, order),
        owner_table.reshape(dp, count),
        left_factor.reshape(factor),
        right_factor.reshape(factor),
        left_root.reshape(factor),
        right_root.reshape(factor),
    )
    return (
        update.reshape(1, count, 1, 1, piece, order),
        new_left.reshape((1, 1) + factor),
        new_right.reshape((1, 1) + factor),
    )


def solution(mesh):
    return jax.shard_map(
        on_device,
        mesh=mesh,
        in_specs=(
            P(("parts", "dp"), None, None, "sub", "own", None, None),
            P("parts", None, None),
            P(("parts", "dp"), "own", None, "sub", None),
            P(("parts", "dp"), "own", None, "sub", None),
            P(("parts", "dp"), "own", None, "sub", None),
            P(("parts", "dp"), "own", None, "sub", None),
        ),
        out_specs=(
            P(("parts", "dp"), None, "sub", "own", None, None),
            P(("parts", "dp"), "own", None, "sub", None),
            P(("parts", "dp"), "own", None, "sub", None),
        ),
        check_vma=False,
    )
```

time: 121 us -> 44.3 us (0.37)
  waiting for transfers between devices: 78.7 us -> 0 us
  Pallas kernels: 0 us -> 35.3 us
  matrix products: 14.4 us -> 0 us
  between operations: 13.8 us -> 0.65 us
  starting transfers between devices: 4.95 us -> 0 us
  local copies, waits for them, and re-layouts: 4.48 us -> 8.03 us
  blocking collectives: 2.46 us -> 0 us
    all_gather x3 -> x0, waiting for transfers between devices: 49.1 us -> none  [the longest x1 28.5 us: on_device(): lax.all_gather(mine[:, None], 'own', axis=1, tiled=True)]
    pallas_call x0 -> x1, Pallas kernels: none -> 35.3 us  [on_device(): pl.pallas_call(functools.partial(kernel, own, dp, sub, count, piece, orde...]
    reduce_scatter x1 -> x0, waiting for transfers between devices: 19 us -> none  [on_device(): lax.psum_scatter(grad_partials.astype(jnp.float32).astype(jnp.bfloat16),...]
    dot_general x6 -> x0, matrix products: 14.4 us -> none  [the longest x1 3.8 us: on_device(): jnp.einsum('srk,skc->src', left_root[0, 0], image, precision=lax.Precisio...]
    all_to_all x1 -> x0, waiting for transfers between devices: 9.87 us -> none  [on_device(): lax.all_to_all(scaled.reshape(slots, peers, piece_rows, order), 'own', sp...]
    unnamed x13, local copies, waits for them, and re-layouts: 1.57 us -> 8.03 us
    all_to_all x1 -> x0, starting transfers between devices: 4.8 us -> none  [on_device(): lax.all_to_all(scaled.reshape(slots, peers, piece_rows, order), 'own', sp...]
    psum x1 -> x0, blocking collectives: 2.46 us -> none  [on_device(): pre_sq = lax.psum(jnp.sum(precond * precond, axis=(1, 2)), 'sub')]
  transfers between devices with their start and end apart: 5 -> 0, of which waited for: 5 -> 0; matrix products, arithmetic and copies ran while one was open for 5% -> 0% of each run, Pallas kernels for 0% -> 0%
where the time goes in v1:
time: 44.3 us; the launch traced here: 44 us
  Pallas kernels  35.3 us (80%)
  local copies, waits for them, and re-layouts  8.03 us (18%)
  between operations  0.65 us (1%)
    pallas_call x1, Pallas kernels, on_device(): pl.pallas_call(functools.partial(kernel, own, dp, sub, count, piece, orde...  35.3 us
    unnamed x13, local copies, waits for them, and re-layouts  8.03 us

profile of v1, /device:TPU:1, one launch (start us, length us, event | category | flops | bytes accessed | tf_op | source)
XLA Modules:
  0.0 44.0 jit_solution(10526755853856378332)
XLA Ops:
  0.6 0.0 copy-start.4
  0.6 0.7 %copy-done.4 = s32[2,4,1]{1,2,0:T(1,128)S(1)} copy-done((s32[2,4,1]{1,2,0:T(1,128)S(1)}, s32[2,4,1]{1,2,0:T(1,128)}, u32[]{:S(2)}) %copy-start.4) | copy-done | bytes 56
  1.3 0.0 copy-start
  1.3 1.2 %copy-done = f32[1,1,2,256,512]{4,3,2,1,0:T(8,128)S(1)} copy-done((f32[1,1,2,256,512]{4,3,2,1,0:T(8,128)S(1)}, f32[1,1,2,256,512]{4,3,2,1,0:T(8,128)}, u32[]{:S(2)}) %copy-start) | copy-done | bytes 1048600
  2.5 0.0 copy-start.1
  2.5 1.2 %copy-done.1 = f32[1,1,2,256,512]{4,3,2,1,0:T(8,128)S(1)} copy-done((f32[1,1,2,256,512]{4,3,2,1,0:T(8,128)S(1)}, f32[1,1,2,256,512]{4,3,2,1,0:T(8,128)}, u32[]{:S(2)}) %copy-start.1) | copy-done | bytes 1048600
  3.8 0.0 copy-start.2
  3.8 1.2 %copy-done.2 = f32[1,1,2,256,512]{4,3,2,1,0:T(8,128)S(1)} copy-done((f32[1,1,2,256,512]{4,3,2,1,0:T(8,128)S(1)}, f32[1,1,2,256,512]{4,3,2,1,0:T(8,128)}, u32[]{:S(2)}) %copy-start.2) | copy-done | bytes 1048600
  5.0 0.0 copy-start.3
  5.0 1.0 %copy-done.3 = bf16[1,2,4,1,1,64,512]{6,5,4,3,2,1,0:T(8,128)(2,1)S(1)} copy-done((bf16[1,2,4,1,1,64,512]{6,5,4,3,2,1,0:T(8,128)(2,1)S(1)}, bf16[1,2,4,1,1,64,512]{6,5,4,3,2,1,0:T(8,128)(2,1)}, u32[]{:S(2)}) %copy-start.3) | copy-done | bytes 524312
  6.0 35.3 %shard_map.85 = (bf16[4,64,512]{2,1,0:T(8,128)(2,1)S(1)}, f32[2,256,512]{2,1,0:T(8,128)S(1)}, f32[2,256,512]{2,1,0:T(8,128)S(1)}) custom-call(bf16[2,4,64,512]{3,2,1,0:T(8,128)(2,1)S(1)} %bitcast.16, s32[2,4]{1,0:T(2,128)S(1)} %bitcast.18, f32[2,256,512]{2,1,0:T(8,128)S(1)} %bitcast.11, f32[2,256,512]{2,1,0:T(8,128)S(1)} %bitcast.12, ...), custom_call_target="tpu_custom_call" | custom-call | tf_op jit(solution)/shard_map/pallas_call | solution.py:254
  41.3 0.7 %copy.13 = bf16[1,4,1,1,64,512]{5,4,3,2,1,0:T(8,128)(2,1)} copy(bf16[1,4,1,1,64,512]{5,4,3,2,1,0:T(8,128)(2,1)S(1)} %bitcast.17) | data formatting | bytes 524288
  42.0 1.0 %copy.14 = f32[1,1,2,256,512]{4,3,2,1,0:T(8,128)} copy(f32[1,1,2,256,512]{4,3,2,1,0:T(8,128)S(1)} %bitcast.15) | data formatting | bytes 2097152
  43.0 1.0 %copy.15 = f32[1,1,2,256,512]{4,3,2,1,0:T(8,128)} copy(f32[1,1,2,256,512]{4,3,2,1,0:T(8,128)S(1)} %bitcast.14) | data formatting | bytes 2097152
Async XLA Ops:
  0.6 0.7 %copy-start.4 = (s32[2,4,1]{1,2,0:T(1,128)S(1)}, s32[2,4,1]{1,2,0:T(1,128)}, u32[]{:S(2)}) copy-start(s32[2,4,1]{1,2,0:T(1,128)} %param.7) | copy-start | bytes 100
  1.3 1.2 %copy-start = (f32[1,1,2,256,512]{4,3,2,1,0:T(8,128)S(1)}, f32[1,1,2,256,512]{4,3,2,1,0:T(8,128)}, u32[]{:S(2)}) copy-start(f32[1,1,2,256,512]{4,3,2,1,0:T(8,128)} %param.8) | copy-start | bytes 3145732
  2.5 1.2 %copy-start.1 = (f32[1,1,2,256,512]{4,3,2,1,0:T(8,128)S(1)}, f32[1,1,2,256,512]{4,3,2,1,0:T(8,128)}, u32[]{:S(2)}) copy-start(f32[1,1,2,256,512]{4,3,2,1,0:T(8,128)} %param.9) | copy-start | bytes 3145732
  3.8 1.2 %copy-start.2 = (f32[1,1,2,256,512]{4,3,2,1,0:T(8,128)S(1)}, f32[1,1,2,256,512]{4,3,2,1,0:T(8,128)}, u32[]{:S(2)}) copy-start(f32[1,1,2,256,512]{4,3,2,1,0:T(8,128)} %param.10) | copy-start | bytes 3145732
  5.0 1.0 %copy-start.3 = (bf16[1,2,4,1,1,64,512]{6,5,4,3,2,1,0:T(8,128)(2,1)S(1)}, bf16[1,2,4,1,1,64,512]{6,5,4,3,2,1,0:T(8,128)(2,1)}, u32[]{:S(2)}) copy-start(bf16[1,2,4,1,1,64,512]{6,5,4,3,2,1,0:T(8,128)(2,1)} %param.6) | copy-start | bytes 1572868

commit v2 on v1

--- a/solution.py
+++ b/solution.py
@@ -9,6 +9,7 @@
 
 BETA = 0.9
 EPS = 1e-06
+PARTS_OUT = 2
 F32 = jnp.float32
 BF16 = jnp.bfloat16
 NT = (((1,), (1,)), ((), ()))
@@ -18,8 +19,9 @@
 
 def kernel(
     own, dp, sub, count, piece, order, slots, chunk,
-    g_hbm, table, lf_hbm, rf_hbm, lr_hbm, rr_hbm,
+    g_hbm, table_hbm, lf_hbm, rf_hbm, lr_hbm, rr_hbm,
     up_ref, nl_hbm, nr_hbm,
+    table,
     g_mine, g_peer, outbox, whole, left, right, left_hi, left_lo, right_hi, right_lo,
     image_hi, image_lo, precond, lf, rf, back, inbox, sq_out, sq_in,
     load_sem, store_sem, dp_send, dp_recv, own_send, own_recv, sub_send, sub_recv,
@@ -40,6 +42,7 @@
         loads.append(copy)
         return copy
 
+    table_load = load(table_hbm, table)
     mine = load(g_hbm.at[me_dp], g_mine)
 
     barrier = pltpu.get_barrier_semaphore()
@@ -62,6 +65,7 @@
     lf_load = load(lf_hbm, lf)
     rf_load = load(rf_hbm, rf)
 
+    table_load.wait()
     owner = [table[me_dp, j] for j in range(count)]
     rank = []
     for j in range(count):
@@ -239,6 +243,19 @@
         copy.wait()
 
 
+def write_out(a, b, c, a_out, b_out, c_out, sem):
+    copies = []
+    for i, (src, dst) in enumerate(((a, a_out), (b, b_out), (c, c_out))):
+        for q in range(PARTS_OUT):
+            step = src.shape[0] // PARTS_OUT
+            rows = pl.ds(q * step, step)
+            copies.append(pltpu.make_async_copy(src.at[rows], dst.at[rows], sem.at[i, q]))
+    for copy in copies:
+        copy.start()
+    for copy in copies:
+        copy.wait()
+
+
 def on_device(grad_partials, owner_table, left_factor, right_factor, left_root, right_root):
     own, dp, sub = lax.axis_size("own"), lax.axis_size("dp"), lax.axis_size("sub")
     count, piece, order = grad_partials.shape[2], grad_partials.shape[5], grad_partials.shape[6]
@@ -248,7 +265,7 @@
     chunks = piece // chunk
     factor = (slots, half, order)
     dma = pltpu.SemaphoreType.DMA
-    hbm, vmem = pl.BlockSpec(memory_space=pl.ANY), pl.BlockSpec(memory_space=pltpu.VMEM)
+    hbm, vmem = pl.BlockSpec(memory_space=pltpu.HBM), pl.BlockSpec(memory_space=pltpu.VMEM)
     peers = max(own - 1, 1)
     twins = max(sub - 1, 1)
     update, new_left, new_right = pl.pallas_call(
@@ -258,9 +275,10 @@
             jax.ShapeDtypeStruct(factor, F32),
             jax.ShapeDtypeStruct(factor, F32),
         ),
-        in_specs=[hbm, pl.BlockSpec(memory_space=pltpu.SMEM), hbm, hbm, hbm, hbm],
+        in_specs=[hbm] * 6,
         out_specs=(vmem, hbm, hbm),
         scratch_shapes=[
+            pltpu.SMEM((dp, count), jnp.int32),
             pltpu.VMEM((count, piece, order), BF16),
             pltpu.VMEM((max(dp - 1, 1), count, piece, order), BF16),
             pltpu.VMEM((slots, peers, piece, order), BF16),
@@ -280,7 +298,7 @@
             pltpu.VMEM((own, slots, sub, piece, half), BF16),
             pltpu.VMEM((slots, 8, 128), F32),
             pltpu.VMEM((slots, twins, 8, 128), F32),
-            dma((5,)),
+            dma((6,)),
             dma((slots, 2)),
             dma((chunks, max(dp - 1, 1))),
             dma((chunks, max(dp - 1, 1))),
@@ -296,7 +314,7 @@
             dma((slots, twins)),
         ],
         compiler_params=pltpu.CompilerParams(
-            collective_id=0, has_side_effects=True, vmem_limit_bytes=48 * 1024 * 1024
+            collective_id=0, has_side_effects=True, vmem_limit_bytes=60 * 1024 * 1024
         ),
     )(
         grad_partials.reshape(dp, count, piece, order),
@@ -306,6 +324,14 @@
         left_root.reshape(factor),
         right_root.reshape(factor),
     )
+    update, new_left, new_right = pl.pallas_call(
+        write_out,
+        out_shape=tuple(jax.ShapeDtypeStruct(x.shape, x.dtype) for x in (update, new_left, new_right)),
+        in_specs=[hbm] * 3,
+        out_specs=(hbm, hbm, hbm),
+        scratch_shapes=[dma((3, PARTS_OUT))],
+        compiler_params=pltpu.CompilerParams(vmem_limit_bytes=8 * 1024 * 1024),
+    )(update, new_left, new_right)
     return (
         update.reshape(1, count, 1, 1, piece, order),
         new_left.reshape((1, 1) + factor),

time: 44.3 us -> 41.4 us (0.935)
  local copies, waits for them, and re-layouts: 8.03 us -> 3.39 us
  Pallas kernels: 35.3 us -> 37.1 us
    unnamed x13 -> x6, local copies, waits for them, and re-layouts: 8.03 us -> 3.39 us
    pallas_call x0 -> x1, Pallas kernels: none -> 1.45 us  [on_device(): pl.pallas_call(write_out, out_shape=tuple((jax.ShapeDtypeStruct(x.shape,...]
where the time goes in v2:
time: 41.4 us; the launch traced here: 41.2 us
  Pallas kernels  37.1 us (90%)
  local copies, waits for them, and re-layouts  3.39 us (8%)
  between operations  0.65 us (2%)
    pallas_call x1, Pallas kernels, on_device(): pl.pallas_call(functools.partial(kernel, own, dp, sub, count, piece, orde...  35.7 us
    unnamed x6, local copies, waits for them, and re-layouts  3.39 us
    pallas_call x1, Pallas kernels, on_device(): pl.pallas_call(write_out, out_shape=tuple((jax.ShapeDtypeStruct(x.shape,...  1.45 us

profile of v2, /device:TPU:1, one launch (start us, length us, event | category | flops | bytes accessed | tf_op | source)
XLA Modules:
  0.0 41.2 jit_solution(7834652319930164424)
XLA Ops:
  0.6 35.7 %shard_map.85 = (bf16[4,64,512]{2,1,0:T(8,128)(2,1)}, f32[2,256,512]{2,1,0:T(8,128)}, f32[2,256,512]{2,1,0:T(8,128)}) custom-call(bf16[2,4,64,512]{3,2,1,0:T(8,128)(2,1)} %bitcast.15, s32[2,4]{1,0:T(2,128)} %bitcast.16, f32[2,256,512]{2,1,0:T(8,128)} %bitcast.11, f32[2,256,512]{2,1,0:T(8,128)} %bitcast.12, f32[2,256,512]{2,1,0:T(8,128)} %bitcast.13, ...), custom_call_target="tpu_custom_call" | custom-call | tf_op jit(solution)/shard_map/pallas_call | solution.py:271
  36.3 0.0 copy-start
  36.3 1.2 %copy-done = f32[2,256,512]{2,1,0:T(8,128)S(1)} copy-done((f32[2,256,512]{2,1,0:T(8,128)S(1)}, f32[2,256,512]{2,1,0:T(8,128)}, u32[]{:S(2)}) %copy-start) | copy-done | bytes 1048600
  37.5 0.0 copy-start.1
  37.5 1.2 %copy-done.1 = f32[2,256,512]{2,1,0:T(8,128)S(1)} copy-done((f32[2,256,512]{2,1,0:T(8,128)S(1)}, f32[2,256,512]{2,1,0:T(8,128)}, u32[]{:S(2)}) %copy-start.1) | copy-done | bytes 1048600
  38.8 0.0 copy-start.2
  38.8 0.9 %copy-done.2 = bf16[4,64,512]{2,1,0:T(8,128)(2,1)S(1)} copy-done((bf16[4,64,512]{2,1,0:T(8,128)(2,1)S(1)}, bf16[4,64,512]{2,1,0:T(8,128)(2,1)}, u32[]{:S(2)}) %copy-start.2) | copy-done | bytes 262168
  39.7 1.4 %shard_map.86 = (bf16[4,64,512]{2,1,0:T(8,128)(2,1)}, f32[2,256,512]{2,1,0:T(8,128)}, f32[2,256,512]{2,1,0:T(8,128)}) custom-call(bf16[4,64,512]{2,1,0:T(8,128)(2,1)S(1)} %copy-done.2, f32[2,256,512]{2,1,0:T(8,128)S(1)} %copy-done, f32[2,256,512]{2,1,0:T(8,128)S(1)} %copy-done.1), custom_call_target="tpu_custom_call" | custom-call | tf_op jit(solution)/shard_map/pallas_call | solution.py:327
Async XLA Ops:
  36.3 1.2 %copy-start = (f32[2,256,512]{2,1,0:T(8,128)S(1)}, f32[2,256,512]{2,1,0:T(8,128)}, u32[]{:S(2)}) copy-start(f32[2,256,512]{2,1,0:T(8,128)} %get-tuple-element.10.b) | copy-start | bytes 3145732
  37.5 1.2 %copy-start.1 = (f32[2,256,512]{2,1,0:T(8,128)S(1)}, f32[2,256,512]{2,1,0:T(8,128)}, u32[]{:S(2)}) copy-start(f32[2,256,512]{2,1,0:T(8,128)} %get-tuple-element.11.c) | copy-start | bytes 3145732
  38.8 0.9 %copy-start.2 = (bf16[4,64,512]{2,1,0:T(8,128)(2,1)S(1)}, bf16[4,64,512]{2,1,0:T(8,128)(2,1)}, u32[]{:S(2)}) copy-start(bf16[4,64,512]{2,1,0:T(8,128)(2,1)} %get-tuple-element.9.a) | copy-start | bytes 786436

commit v3 on v2

--- a/solution.py
+++ b/solution.py
@@ -330,7 +330,7 @@
         in_specs=[hbm] * 3,
         out_specs=(hbm, hbm, hbm),
         scratch_shapes=[dma((3, PARTS_OUT))],
-        compiler_params=pltpu.CompilerParams(vmem_limit_bytes=8 * 1024 * 1024),
+        compiler_params=pltpu.CompilerParams(vmem_limit_bytes=60 * 1024 * 1024),
     )(update, new_left, new_right)
     return (
         update.reshape(1, count, 1, 1, piece, order),

time: 41.4 us -> 109 us (2.63)
  Pallas kernels: 37.1 us -> 108 us
  local copies, waits for them, and re-layouts: 3.39 us -> 0 us
    pallas_call x1, Pallas kernels: 1.45 us -> 72.6 us  [on_device(): pl.pallas_call(write_out, out_shape=tuple((jax.ShapeDtypeStruct(x.shape,...]
    unnamed x6 -> x0, local copies, waits for them, and re-layouts: 3.39 us -> none
where the time goes in v3:
time: 109 us
  Pallas kernels  108 us (99%)
    pallas_call x1, Pallas kernels, on_device(): pl.pallas_call(write_out, out_shape=tuple((jax.ShapeDtypeStruct(x.shape,...  72.6 us
    pallas_call x1, Pallas kernels, on_device(): pl.pallas_call(functools.partial(kernel, own, dp, sub, count, piece, orde...  35.7 us

profile of v3, /device:TPU:1, one launch (start us, length us, event | category | flops | bytes accessed | tf_op | source)
XLA Modules:
  0.0 109.0 jit_solution(2068009732238579554)
XLA Ops:
  0.6 35.7 %shard_map.85 = (bf16[4,64,512]{2,1,0:T(8,128)(2,1)}, f32[2,256,512]{2,1,0:T(8,128)}, f32[2,256,512]{2,1,0:T(8,128)}) custom-call(bf16[2,4,64,512]{3,2,1,0:T(8,128)(2,1)} %bitcast.15, s32[2,4]{1,0:T(2,128)} %bitcast.16, f32[2,256,512]{2,1,0:T(8,128)} %bitcast.11, f32[2,256,512]{2,1,0:T(8,128)} %bitcast.12, f32[2,256,512]{2,1,0:T(8,128)} %bitcast.13, ...), custom_call_target="tpu_custom_call" | custom-call | tf_op jit(solution)/shard_map/pallas_call | solution.py:271
  36.3 72.6 %shard_map.86 = (bf16[4,64,512]{2,1,0:T(8,128)(2,1)}, f32[2,256,512]{2,1,0:T(8,128)}, f32[2,256,512]{2,1,0:T(8,128)}) custom-call(bf16[4,64,512]{2,1,0:T(8,128)(2,1)} %get-tuple-element.9.a, f32[2,256,512]{2,1,0:T(8,128)} %get-tuple-element.10.b, f32[2,256,512]{2,1,0:T(8,128)} %get-tuple-element.11.c), custom_call_target="tpu_custom_call" | custom-call | tf_op jit(solution)/shard_map/pallas_call | solution.py:327

commit v4 on v3

--- a/solution.py
+++ b/solution.py
@@ -9,7 +9,7 @@
 
 BETA = 0.9
 EPS = 1e-06
-PARTS_OUT = 2
+PARTS_OUT = 1
 F32 = jnp.float32
 BF16 = jnp.bfloat16
 NT = (((1,), (1,)), ((), ()))
@@ -243,17 +243,22 @@
         copy.wait()
 
 
-def write_out(a, b, c, a_out, b_out, c_out, sem):
-    copies = []
-    for i, (src, dst) in enumerate(((a, a_out), (b, b_out), (c, c_out))):
-        for q in range(PARTS_OUT):
-            step = src.shape[0] // PARTS_OUT
-            rows = pl.ds(q * step, step)
-            copies.append(pltpu.make_async_copy(src.at[rows], dst.at[rows], sem.at[i, q]))
-    for copy in copies:
-        copy.start()
-    for copy in copies:
-        copy.wait()
+def write_out(a, b, c, a_out, b_out, c_out, a_held, b_held, c_held, in_sem, out_sem):
+    ins, outs = [], []
+    for i, (src, held, dst) in enumerate(((b, b_held, b_out), (c, c_held, c_out), (a, a_held, a_out))):
+        step = src.shape[1] // PARTS_OUT
+        for lead in range(src.shape[0]):
+            for q in range(PARTS_OUT):
+                at = (lead, pl.ds(q * step, step))
+                n = len(ins)
+                ins.append(pltpu.make_async_copy(src.at[at], held.at[at], in_sem.at[n]))
+                outs.append(pltpu.make_async_copy(held.at[at], dst.at[at], out_sem.at[n]))
+                ins[-1].start()
+    for load, store in zip(ins, outs):
+        load.wait()
+        store.start()
+    for store in outs:
+        store.wait()
 
 
 def on_device(grad_partials, owner_table, left_factor, right_factor, left_root, right_root):
@@ -329,7 +334,8 @@
         out_shape=tuple(jax.ShapeDtypeStruct(x.shape, x.dtype) for x in (update, new_left, new_right)),
         in_specs=[hbm] * 3,
         out_specs=(hbm, hbm, hbm),
-        scratch_shapes=[dma((3, PARTS_OUT))],
+        scratch_shapes=[pltpu.VMEM(x.shape, x.dtype) for x in (update, new_left, new_right)]
+        + [dma(((count + 2 * slots) * PARTS_OUT,))] * 2,
         compiler_params=pltpu.CompilerParams(vmem_limit_bytes=60 * 1024 * 1024),
     )(update, new_left, new_right)
     return (

time: 109 us -> 39.1 us (0.36)
  Pallas kernels: 108 us -> 38.3 us
    pallas_call x1, Pallas kernels: 72.6 us -> 2.57 us  [on_device(): pl.pallas_call(write_out, out_shape=tuple((jax.ShapeDtypeStruct(x.shape,...]
where the time goes in v4:
time: 39.1 us; the launch traced here: 38.9 us
  Pallas kernels  38.3 us (98%)
  between operations  0.64 us (2%)
    pallas_call x1, Pallas kernels, on_device(): pl.pallas_call(functools.partial(kernel, own, dp, sub, count, piece, orde...  35.7 us
    pallas_call x1, Pallas kernels, on_device(): pl.pallas_call(write_out, out_shape=tuple((jax.ShapeDtypeStruct(x.shape,...  2.57 us

profile of v4, /device:TPU:1, one launch (start us, length us, event | category | flops | bytes accessed | tf_op | source)
XLA Modules:
  0.0 38.9 jit_solution(12137916139502229520)
XLA Ops:
  0.6 35.7 %shard_map.85 = (bf16[4,64,512]{2,1,0:T(8,128)(2,1)}, f32[2,256,512]{2,1,0:T(8,128)}, f32[2,256,512]{2,1,0:T(8,128)}) custom-call(bf16[2,4,64,512]{3,2,1,0:T(8,128)(2,1)} %bitcast.15, s32[2,4]{1,0:T(2,128)} %bitcast.16, f32[2,256,512]{2,1,0:T(8,128)} %bitcast.11, f32[2,256,512]{2,1,0:T(8,128)} %bitcast.12, f32[2,256,512]{2,1,0:T(8,128)} %bitcast.13, ...), custom_call_target="tpu_custom_call" | custom-call | tf_op jit(solution)/shard_map/pallas_call | solution.py:276
  36.3 2.6 %shard_map.86 = (bf16[4,64,512]{2,1,0:T(8,128)(2,1)}, f32[2,256,512]{2,1,0:T(8,128)}, f32[2,256,512]{2,1,0:T(8,128)}) custom-call(bf16[4,64,512]{2,1,0:T(8,128)(2,1)} %get-tuple-element.9.a, f32[2,256,512]{2,1,0:T(8,128)} %get-tuple-element.10.b, f32[2,256,512]{2,1,0:T(8,128)} %get-tuple-element.11.c), custom_call_target="tpu_custom_call" | custom-call | tf_op jit(solution)/shard_map/pallas_call | solution.py:332
